TPU v7x, 512 devices: a whole 4x8x8 slice. The times are simulated.
512 devices in a mesh: gx: 64 (over y, z), gy: 8 (over x, core).
Axes of the slice: x: 4, y: 8, z: 8, core: 2. Of those that a mesh axis runs over, the one named last changes fastest.
Arguments:
- load_field: float32 [128, 32, 128, 256], P('gx', 'gy'), may hold values from -6 to 6
- schur_blocks: bfloat16 [128, 32, 256, 256], P('gx', 'gy'), may hold values from -1 to 10, as said below
- local_inverse: bfloat16 [128, 32, 256, 256], P('gx', 'gy'), may hold values from -1 to 10, as said below
- face_order: int32 [128, 32, 2, 64], P('gx', 'gy'), may hold values from 0 to 63, each once within a row
- coarse_weights: float32 [128], replicated, may hold values from 0.03 to 0.12
- coarse_decay: float32 [128, 32], P('gx', 'gy'), may hold values from 0.00390625 to 0.0390625
Outputs:
- solution_field: float32 [128, 32, 128, 256], P('gx', 'gy')
Inputs may be any that keep to these rules, and one draw needn't show every extreme that they name: `schur_blocks`: every block is symmetric positive definite. `local_inverse`: every block is symmetric positive definite. `face_order`: each row of 64 numbers holds every number of 0 to 63 once.
All inputs are finite; a program needn't handle non-finite values.
Results may differ from a plain program's by a relative error of at most 0.0022.
Values may be sent and summed in bfloat16 or wider, within the bound.
A program may use at most 64 MiB of HBM per device.

v0:
```python
import jax
import jax.numpy as jnp
from jax import lax
from jax.sharding import PartitionSpec as P

SUB_X = 2
SUB_Y = 4
ITERS = 2


def shifted(value, axis, by):
    count = lax.axis_size(axis)
    pairs = [(i, i + by) for i in range(count) if 0 <= i + by < count]
    return lax.ppermute(value, axis, pairs)


def edge_open(face_count):
    grid_x = SUB_X * lax.axis_size("gx")
    grid_y = SUB_Y * lax.axis_size("gy")
    first_index = lax.axis_index("gx") * SUB_X + jnp.arange(SUB_X, dtype=jnp.int32)
    second_index = lax.axis_index("gy") * SUB_Y + jnp.arange(SUB_Y, dtype=jnp.int32)
    first_open = (first_index < grid_x - 1).astype(jnp.float32)
    second_open = (second_index < grid_y - 1).astype(jnp.float32)
    east_open = jnp.broadcast_to(first_open[:, None, None, None], (SUB_X, SUB_Y, face_count, 1))
    north_open = jnp.broadcast_to(second_open[None, :, None, None], (SUB_X, SUB_Y, face_count, 1))
    return jnp.concatenate([east_open, north_open], axis=2)


def assemble(values, blocks, hot_low, hot_high):
    face_count = hot_low.shape[-1]
    east_face = values[:, :, :face_count]
    north_face = values[:, :, face_count:]
    from_west = shifted(east_face[-1:], "gx", 1)
    from_south = shifted(north_face[:, -1:], "gy", 1)
    west_raw = jnp.concatenate([from_west, east_face[:-1]], axis=0)
    south_raw = jnp.concatenate([from_south, north_face[:, :-1]], axis=1)
    west_face = jnp.einsum(
        "xyji,xyir->xyjr", hot_low[:, :, 0], west_raw, preferred_element_type=jnp.float32
    ).astype(jnp.bfloat16)
    south_face = jnp.einsum(
        "xyji,xyir->xyjr", hot_low[:, :, 1], south_raw, preferred_element_type=jnp.float32
    ).astype(jnp.bfloat16)
    local_part = jnp.concatenate([east_face, north_face, west_face, south_face], axis=2)
    image_part = jnp.einsum(
        "xyij,xyjr->xyir", blocks, local_part, preferred_element_type=jnp.float32
    )
    back_west = jnp.einsum(
        "xyji,xyjr->xyir",
        hot_high[:, :, 0],
        image_part[:, :, 2 * face_count : 3 * face_count],
        precision=lax.Precision.HIGHEST,
    )
    back_south = jnp.einsum(
        "xyji,xyjr->xyir",
        hot_high[:, :, 1],
        image_part[:, :, 3 * face_count :],
        precision=lax.Precision.HIGHEST,
    )
    from_east = shifted(back_west[:1].astype(jnp.bfloat16), "gx", -1).astype(jnp.float32)
    from_north = shifted(back_south[:, :1].astype(jnp.bfloat16), "gy", -1).astype(jnp.float32)
    east_total = image_part[:, :, :face_count] + jnp.concatenate([back_west[1:], from_east], axis=0)
    north_total = image_part[:, :, face_count : 2 * face_count] + jnp.concatenate(
        [back_south[:, 1:], from_north], axis=1
    )
    return (jnp.concatenate([east_total, north_total], axis=2), local_part, image_part)


def line_solve(whole_decay, whole_demand):
    line_length = whole_decay.shape[0]
    running = jnp.cumsum(whole_decay, axis=0)
    spacing = running[None, :, :] - running[:, None, :]
    position = jnp.arange(line_length, dtype=jnp.int32)
    below = position[:, None] >= position[None, :]
    transfer = jnp.where(below[:, :, None], jnp.exp(jnp.minimum(spacing, 0.0)), 0.0)
    climbed = jnp.einsum("asy,syr->ayr", transfer, whole_demand, precision=lax.Precision.HIGHEST)
    return jnp.einsum("tay,tyr->ayr", transfer, climbed, precision=lax.Precision.HIGHEST)


def coarse_values(residual_field, weights, decay):
    demand = jnp.einsum("k,xykr->xyr", weights, residual_field, precision=lax.Precision.HIGHEST)
    whole_demand, whole_decay = (
        lax.all_gather(demand, "gx", axis=0, tiled=True),
        lax.all_gather(decay, "gx", axis=0, tiled=True),
    )
    settled_all = line_solve(whole_decay, whole_demand)
    first_row = lax.axis_index("gx") * SUB_X
    return lax.dynamic_slice_in_dim(settled_all, first_row, SUB_X, 0)


def precondition(residual_field, inverse_blocks, hot_low, hot_high, weights, decay, opened):
    halved = (0.5 * residual_field).astype(jnp.bfloat16)
    assembled = assemble(halved, inverse_blocks, hot_low, hot_high)[0]
    settled = coarse_values(residual_field, weights, decay)
    return opened * (0.5 * assembled + weights[None, None, :, None] * settled[:, :, None, :])


def global_inner(residual_field, smoothed):
    return lax.psum(jnp.sum(residual_field * smoothed, axis=(0, 1, 2)), ("gx", "gy"))


def local(load_field, schur_blocks, local_inverse, face_order, coarse_weights, coarse_decay):
    face_count = face_order.shape[-1]
    opened = edge_open(face_count)
    hot_high = (face_order[..., :, None] == jnp.arange(face_count, dtype=jnp.int32)).astype(
        jnp.float32
    )
    hot_low = hot_high.astype(jnp.bfloat16)
    residual_field = opened * load_field
    solution_field = jnp.zeros_like(load_field)
    search = precondition(
        residual_field, local_inverse, hot_low, hot_high, coarse_weights, coarse_decay, opened
    )
    inner_now = global_inner(residual_field, search)
    for number in range(ITERS):
        rounded = search.astype(jnp.bfloat16)
        assembled, local_part, image_part = assemble(rounded, schur_blocks, hot_low, hot_high)
        product = opened * assembled
        curvature = lax.psum(
            jnp.sum(rounded.astype(jnp.float32) * product, axis=(0, 1, 2)), ("gx", "gy")
        )
        step_size = inner_now / curvature
        solution_field = solution_field + step_size * search
        residual_field = residual_field - step_size * product
        if number + 1 < ITERS:
            smoothed = precondition(
                residual_field,
                local_inverse,
                hot_low,
                hot_high,
                coarse_weights,
                coarse_decay,
                opened,
            )
            inner_next = global_inner(residual_field, smoothed)
            search = smoothed + inner_next / inner_now * search
            inner_now = inner_next
    return solution_field


def solution(mesh):
    in_specs = (
        P("gx", "gy", None, None),
        P("gx", "gy", None, None),
        P("gx", "gy", None, None),
        P("gx", "gy", None, None),
        P(),
        P("gx", "gy"),
    )
    out_specs = P("gx", "gy", None, None)
    return jax.shard_map(local, mesh=mesh, in_specs=in_specs, out_specs=out_specs, check_vma=False)
```

profile of v0, /device:TPU:1, one launch (start us, length us, event | category | flops | bytes accessed | tf_op | source)
XLA Modules:
  0.0 537.8 jit_solution(7932301347020105250)
XLA Ops:
  0.3 1.6 multiply_convert_fusion.1
  2.5 4.5 collective-permute-start.1
  7.7 4.6 collective-permute-start
  13.8 41.5 %all-gather = f32[64,2,4]{2,1,0:T(2,128)S(1)} all-gather(f32[1,2,4]{2,1,0:T(2,128)S(1)} %bitcast.69), channel_id=1, replica_groups=mesh['gx'=64,'gy'=8] {'gx'}, dimensions={0}, use_global_device_ids=true | all-gather | bytes 2080 | tf_op jit(solution)/shard_map/all_gather | solution.py:83
  55.6 35.8 %all_gather.10 = f32[128,4,256]{2,1,0:T(4,128)S(1)} all-gather(f32[2,4,256]{2,1,0:T(4,128)S(1)} %bitcast.68), channel_id=1, replica_groups=mesh['gx'=64,'gy'=8] {'gx'}, dimensions={0}, use_global_device_ids=true | all-gather | bytes 532480 | tf_op jit(solution)/shard_map/all_gather | solution.py:82
  92.2 1.4 fusion.72
  97.0 1.3 collective-permute-start.2
  98.8 25.9 %collective-permute-start.3 = (bf16[2,1,64,256]{3,2,1,0:T(8,128)(2,1)S(1)}, bf16[2,1,64,256]{3,2,1,0:T(8,128)(2,1)S(1)}, u32[]{:S(2)}, u32[]{:S(2)}) collective-permute-start(bf16[2,1,64,256]{3,2,1,0:T(8,128)(2,1)S(1)} %slice.367), channel_id=1, source_target_pairs={{1,0},{2,1},{3,2},{4,3},{5,4},{6,5},{7,6},{9,8},{10,9},{11,10},{12... | collective-permute-start | bytes 196616 | tf_op jit(solution)/shard_map/ppermute | solution.py:14
  125.6 2.0 collective-permute-done.3
  128.1 3.0 collective-permute-start.5
  131.1 3.0 collective-permute-start.4
  134.5 2.1 collective-permute-done.4
  137.7 1.3 collective-permute-start.6
  139.4 3.2 collective-permute-start.7
  142.7 3.2 collective-permute-done.7
  147.2 101.1 %all-reduce = (f32[256]{0:T(256)}, f32[256]{0:T(256)}) all-reduce(f32[256]{0:T(256)} %get-tuple-element.6, f32[256]{0:T(256)} %get-tuple-element.5), channel_id=1, replica_groups=mesh['gx'=64,'gy'=8] {'gx','gy'}, use_global_device_ids=true, to_apply=%region_2.3 | all-reduce | flops 512 | bytes 4096 | tf_op jit(solution)/shard_map/psum | solution.py:98
  249.0 1.5 multiply_convert_fusion
  251.2 4.1 collective-permute-start.9
  255.3 2.7 collective-permute-start.8
  258.0 37.6 %all_gather.12 = f32[128,4,256]{2,1,0:T(4,128)S(1)} all-gather(f32[2,4,256]{2,1,0:T(4,128)S(1)} %bitcast.67), channel_id=1, replica_groups=mesh['gx'=64,'gy'=8] {'gx'}, dimensions={0}, use_global_device_ids=true | all-gather | bytes 532480 | tf_op jit(solution)/shard_map/all_gather | solution.py:82
  298.5 1.3 collective-permute-start.10
  300.3 12.3 %collective-permute-start.11 = (bf16[2,1,64,256]{3,2,1,0:T(8,128)(2,1)S(1)}, bf16[2,1,64,256]{3,2,1,0:T(8,128)(2,1)S(1)}, u32[]{:S(2)}, u32[]{:S(2)}) collective-permute-start(bf16[2,1,64,256]{3,2,1,0:T(8,128)(2,1)S(1)} %slice.365), channel_id=1, source_target_pairs={{1,0},{2,1},{3,2},{4,3},{5,4},{6,5},{7,6},{9,8},{10,9},{11,10},{12... | collective-permute-start | bytes 196616 | tf_op jit(solution)/shard_map/ppermute | solution.py:14
  312.7 3.4 collective-permute-done.11
  317.3 98.2 %psum.30 = f32[256]{0:T(256)} all-reduce(f32[256]{0:T(256)} %multiply_reduce_fusion), channel_id=1, replica_groups=mesh['gx'=64,'gy'=8] {'gx','gy'}, use_global_device_ids=true, to_apply=%region_6.7 | all-reduce | flops 256 | bytes 2048 | tf_op jit(solution)/shard_map/psum | solution.py:98
  417.5 4.2 collective-permute-start.13
  421.8 3.3 collective-permute-start.12
  425.3 1.7 collective-permute-done.12
  428.1 1.3 collective-permute-start.14
  429.9 1.9 collective-permute-start.15
  431.8 3.6 collective-permute-done.15
  435.9 99.1 %psum.31 = f32[256]{0:T(256)S(1)} all-reduce(f32[256]{0:T(256)S(1)} %fusion.25), channel_id=1, replica_groups=mesh['gx'=64,'gy'=8] {'gx','gy'}, use_global_device_ids=true, to_apply=%region_8.9 | all-reduce | flops 256 | bytes 2048 | tf_op jit(solution)/shard_map/psum | solution.py:118
  535.6 2.2 multiply_add_fusion
  (145 shorter events, 22.9 us)
Async XLA Ops:
  0.0 96.2 %copy-start = (bf16[2,4,256,256]{3,2,1,0:T(8,128)(2,1)S(1)}, bf16[2,4,256,256]{3,2,1,0:T(8,128)(2,1)}, u32[]{:S(2)}) copy-start(bf16[2,4,256,256]{3,2,1,0:T(8,128)(2,1)} %param.8) | copy-start | bytes 3145732
  0.0 12.4 %copy-start.1 = (f32[2,4,128,256]{3,2,1,0:T(8,128)S(1)}, f32[2,4,128,256]{3,2,1,0:T(8,128)}, u32[]{:S(2)}) copy-start(f32[2,4,128,256]{3,2,1,0:T(8,128)} %param.6) | copy-start | bytes 3145732
  0.0 12.4 %copy-start.15 = (f32[128]{0:T(128)S(1)}, f32[128]{0:T(128)}, u32[]{:S(2)}) copy-start(f32[128]{0:T(128)} %param.10) | copy-start | bytes 1540
  0.0 13.2 %copy-start.21 = (s32[2,4,2,64]{3,2,1,0:T(2,128)S(1)}, s32[2,4,2,64]{3,2,1,0:T(2,128)}, u32[]{:S(2)}) copy-start(s32[2,4,2,64]{3,2,1,0:T(2,128)} %param.9) | copy-start | bytes 12292
  0.0 13.8 %copy-start.22 = (f32[2,4]{1,0:T(2,128)S(1)}, f32[2,4]{1,0:T(2,128)}, u32[]{:S(2)}) copy-start(f32[2,4]{1,0:T(2,128)} %param.11) | copy-start | bytes 100
  0.3 91.9 %copy-start.6 = (f32[2,4,128]{2,1,0:T(4,128)}, f32[2,4,128]{2,1,0:T(4,128)S(1)}, u32[]{:S(2)}) copy-start(f32[2,4,128]{2,1,0:T(4,128)S(1)} %maximum_bitcast_fusion) | copy-start | bytes 12292
  2.5 91.3 %collective-permute-start.1 = (bf16[2,1,64,256]{3,2,1,0:T(8,128)(2,1)}, bf16[2,1,64,256]{3,2,1,0:T(8,128)(2,1)}, u32[]{:S(2)}, u32[]{:S(2)}) collective-permute-start(bf16[2,1,64,256]{3,2,1,0:T(8,128)(2,1)} %slice.260), channel_id=1, source_target_pairs={{0,1},{1,2},{2,3},{3,4},{4,5},{5,6},{6,7},{8,9},{9,10},{10,11},{11... | collective-permute-start | bytes 196616 | tf_op jit(solution)/shard_map/ppermute | solution.py:14
  7.7 87.2 %collective-permute-start = (bf16[1,4,64,256]{3,2,1,0:T(8,128)(2,1)}, bf16[1,4,64,256]{3,2,1,0:T(8,128)(2,1)}, u32[]{:S(2)}, u32[]{:S(2)}) collective-permute-start(bf16[1,4,64,256]{3,2,1,0:T(8,128)(2,1)} %get-tuple-element.25), channel_id=1, source_target_pairs={{0,8},{8,16},{16,24},{24,32},{32,40},{40,48},{48,56},{56,64},{64,7... | collective-permute-start | bytes 393224 | tf_op jit(solution)/shard_map/ppermute | solution.py:14
  55.6 36.6 %copy-start.11 = (f32[128,4]{0,1:T(4,128)}, f32[128,4]{0,1:T(4,128)S(1)}, u32[]{:S(2)}) copy-start(f32[128,4]{0,1:T(4,128)S(1)} %copy.13) | copy-start | bytes 6148
  55.6 38.1 %copy-start.14 = (s32[2,4,2,64]{3,1,0,2:T(4,128)S(1)}, s32[2,4,2,64]{3,1,0,2:T(4,128)}, u32[]{:S(2)}) copy-start(s32[2,4,2,64]{3,1,0,2:T(4,128)} %copy.12) | copy-start | bytes 12292
  97.0 30.5 %collective-permute-start.2 = (bf16[1,4,64,256]{3,2,1,0:T(8,128)(2,1)S(1)}, bf16[1,4,64,256]{3,2,1,0:T(8,128)(2,1)S(1)}, u32[]{:S(2)}, u32[]{:S(2)}) collective-permute-start(bf16[1,4,64,256]{3,2,1,0:T(8,128)(2,1)S(1)} %slice.363), channel_id=1, source_target_pairs={{8,0},{16,8},{24,16},{32,24},{40,32},{48,40},{56,48},{64,56},{72,6... | collective-permute-start | bytes 393224 | tf_op jit(solution)/shard_map/ppermute | solution.py:14
  98.8 28.8 %collective-permute-start.3 = (bf16[2,1,64,256]{3,2,1,0:T(8,128)(2,1)S(1)}, bf16[2,1,64,256]{3,2,1,0:T(8,128)(2,1)S(1)}, u32[]{:S(2)}, u32[]{:S(2)}) collective-permute-start(bf16[2,1,64,256]{3,2,1,0:T(8,128)(2,1)S(1)} %slice.367), channel_id=1, source_target_pairs={{1,0},{2,1},{3,2},{4,3},{5,4},{6,5},{7,6},{9,8},{10,9},{11,10},{12... | collective-permute-start | bytes 196616 | tf_op jit(solution)/shard_map/ppermute | solution.py:14
  125.5 20.7 %copy-start.9 = (f32[2,4,256]{2,1,0:T(4,128)}, f32[2,4,256]{2,1,0:T(4,128)S(1)}, u32[]{:S(2)}) copy-start(f32[2,4,256]{2,1,0:T(4,128)S(1)} %copy.15) | copy-start | bytes 24580
  127.7 9.1 %copy-start.4 = (bf16[2,4,256,256]{3,2,1,0:T(8,128)(2,1)S(1)}, bf16[2,4,256,256]{3,2,1,0:T(8,128)(2,1)}, u32[]{:S(2)}) copy-start(bf16[2,4,256,256]{3,2,1,0:T(8,128)(2,1)} %param.7) | copy-start | bytes 3145732
  128.1 6.1 %collective-permute-start.5 = (bf16[2,1,64,256]{3,2,1,0:T(8,128)(2,1)S(1)}, bf16[2,1,64,256]{3,2,1,0:T(8,128)(2,1)S(1)}, u32[]{:S(2)}, u32[]{:S(2)}) collective-permute-start(bf16[2,1,64,256]{3,2,1,0:T(8,128)(2,1)S(1)} %slice.274), channel_id=1, source_target_pairs={{0,1},{1,2},{2,3},{3,4},{4,5},{5,6},{6,7},{8,9},{9,10},{10,11},{11... | collective-permute-start | bytes 196616 | tf_op jit(solution)/shard_map/ppermute | solution.py:14
  131.1 5.4 collective-permute-start.4
  137.7 8.3 %collective-permute-start.6 = (bf16[1,4,64,256]{3,2,1,0:T(8,128)(2,1)S(1)}, bf16[1,4,64,256]{3,2,1,0:T(8,128)(2,1)S(1)}, u32[]{:S(2)}, u32[]{:S(2)}) collective-permute-start(bf16[1,4,64,256]{3,2,1,0:T(8,128)(2,1)S(1)} %slice.362), channel_id=1, source_target_pairs={{8,0},{16,8},{24,16},{32,24},{40,32},{48,40},{56,48},{64,56},{72,6... | collective-permute-start | bytes 393224 | tf_op jit(solution)/shard_map/ppermute | solution.py:14
  139.4 6.5 %collective-permute-start.7 = (bf16[2,1,64,256]{3,2,1,0:T(8,128)(2,1)S(1)}, bf16[2,1,64,256]{3,2,1,0:T(8,128)(2,1)S(1)}, u32[]{:S(2)}, u32[]{:S(2)}) collective-permute-start(bf16[2,1,64,256]{3,2,1,0:T(8,128)(2,1)S(1)} %slice.366), channel_id=1, source_target_pairs={{1,0},{2,1},{3,2},{4,3},{5,4},{6,5},{7,6},{9,8},{10,9},{11,10},{12... | collective-permute-start | bytes 196616 | tf_op jit(solution)/shard_map/ppermute | solution.py:14
  249.0 46.6 %copy-start.12 = (f32[128,4]{0,1:T(4,128)S(1)}, f32[128,4]{0,1:T(4,128)}, u32[]{:S(2)}) copy-start(f32[128,4]{0,1:T(4,128)} %copy-done.11) | copy-start | bytes 6148
  251.2 45.9 %collective-permute-start.9 = (bf16[2,1,64,256]{3,2,1,0:T(8,128)(2,1)S(1)}, bf16[2,1,64,256]{3,2,1,0:T(8,128)(2,1)S(1)}, u32[]{:S(2)}, u32[]{:S(2)}) collective-permute-start(bf16[2,1,64,256]{3,2,1,0:T(8,128)(2,1)S(1)} %slice.286), channel_id=1, source_target_pairs={{0,1},{1,2},{2,3},{3,4},{4,5},{5,6},{6,7},{8,9},{9,10},{10,11},{11... | collective-permute-start | bytes 196616 | tf_op jit(solution)/shard_map/ppermute | solution.py:14
  255.3 42.1 %collective-permute-start.8 = (bf16[1,4,64,256]{3,2,1,0:T(8,128)(2,1)S(1)}, bf16[1,4,64,256]{3,2,1,0:T(8,128)(2,1)S(1)}, u32[]{:S(2)}, u32[]{:S(2)}) collective-permute-start(bf16[1,4,64,256]{3,2,1,0:T(8,128)(2,1)S(1)} %get-tuple-element.21), channel_id=1, source_target_pairs={{0,8},{8,16},{16,24},{24,32},{32,40},{40,48},{48,56},{56,64},{64,7... | collective-permute-start | bytes 393224 | tf_op jit(solution)/shard_map/ppermute | solution.py:14
  298.5 17.6 %collective-permute-start.10 = (bf16[1,4,64,256]{3,2,1,0:T(8,128)(2,1)S(1)}, bf16[1,4,64,256]{3,2,1,0:T(8,128)(2,1)S(1)}, u32[]{:S(2)}, u32[]{:S(2)}) collective-permute-start(bf16[1,4,64,256]{3,2,1,0:T(8,128)(2,1)S(1)} %slice.361), channel_id=1, source_target_pairs={{8,0},{16,8},{24,16},{32,24},{40,32},{48,40},{56,48},{64,56},{72,6... | collective-permute-start | bytes 393224 | tf_op jit(solution)/shard_map/ppermute | solution.py:14
  300.3 15.9 %collective-permute-start.11 = (bf16[2,1,64,256]{3,2,1,0:T(8,128)(2,1)S(1)}, bf16[2,1,64,256]{3,2,1,0:T(8,128)(2,1)S(1)}, u32[]{:S(2)}, u32[]{:S(2)}) collective-permute-start(bf16[2,1,64,256]{3,2,1,0:T(8,128)(2,1)S(1)} %slice.365), channel_id=1, source_target_pairs={{1,0},{2,1},{3,2},{4,3},{5,4},{6,5},{7,6},{9,8},{10,9},{11,10},{12... | collective-permute-start | bytes 196616 | tf_op jit(solution)/shard_map/ppermute | solution.py:14
  312.6 3.7 copy-start.13
  312.7 3.7 copy-start.8
  316.2 100.0 %copy-start.10 = (f32[2,4,256]{2,1,0:T(4,128)S(1)}, f32[2,4,256]{2,1,0:T(4,128)}, u32[]{:S(2)}) copy-start(f32[2,4,256]{2,1,0:T(4,128)} %copy-done.9) | copy-start | bytes 24580
  316.2 100.0 %copy-start.18 = (f32[128]{0:T(128)S(1)}, f32[128]{0:T(128)}, u32[]{:S(2)}) copy-start(f32[128]{0:T(128)} %param.10) | copy-start | bytes 1540
  416.2 11.1 %copy-start.5 = (bf16[2,4,256,256]{3,2,1,0:T(8,128)(2,1)S(1)}, bf16[2,4,256,256]{3,2,1,0:T(8,128)(2,1)}, u32[]{:S(2)}) copy-start(bf16[2,4,256,256]{3,2,1,0:T(8,128)(2,1)} %param.7) | copy-start | bytes 3145732
  417.5 7.6 %collective-permute-start.13 = (bf16[2,1,64,256]{3,2,1,0:T(8,128)(2,1)S(1)}, bf16[2,1,64,256]{3,2,1,0:T(8,128)(2,1)S(1)}, u32[]{:S(2)}, u32[]{:S(2)}) collective-permute-start(bf16[2,1,64,256]{3,2,1,0:T(8,128)(2,1)S(1)} %slice.298), channel_id=1, source_target_pairs={{0,1},{1,2},{2,3},{3,4},{4,5},{5,6},{6,7},{8,9},{9,10},{10,11},{11... | collective-permute-start | bytes 196616 | tf_op jit(solution)/shard_map/ppermute | solution.py:14
  421.8 5.2 collective-permute-start.12
  428.1 7.3 %collective-permute-start.14 = (bf16[1,4,64,256]{3,2,1,0:T(8,128)(2,1)S(1)}, bf16[1,4,64,256]{3,2,1,0:T(8,128)(2,1)S(1)}, u32[]{:S(2)}, u32[]{:S(2)}) collective-permute-start(bf16[1,4,64,256]{3,2,1,0:T(8,128)(2,1)S(1)} %slice.360), channel_id=1, source_target_pairs={{8,0},{16,8},{24,16},{32,24},{40,32},{48,40},{56,48},{64,56},{72,6... | collective-permute-start | bytes 393224 | tf_op jit(solution)/shard_map/ppermute | solution.py:14
  429.9 5.6 %collective-permute-start.15 = (bf16[2,1,64,256]{3,2,1,0:T(8,128)(2,1)S(1)}, bf16[2,1,64,256]{3,2,1,0:T(8,128)(2,1)S(1)}, u32[]{:S(2)}, u32[]{:S(2)}) collective-permute-start(bf16[2,1,64,256]{3,2,1,0:T(8,128)(2,1)S(1)} %slice.364), channel_id=1, source_target_pairs={{1,0},{2,1},{3,2},{4,3},{5,4},{6,5},{7,6},{9,8},{10,9},{11,10},{12... | collective-permute-start | bytes 196616 | tf_op jit(solution)/shard_map/ppermute | solution.py:14
  (7 other events, 11.0 us)
where the time goes:
time: 539 us; the launch traced here: 538 us
  blocking collectives  413 us (77%)
  starting transfers between devices  78.1 us (14%)
  waiting for transfers between devices  15.9 us (3%)
  matrix products  14 us (3%)
  other arithmetic  12.1 us (2%)
    psum x2, blocking collectives, global_inner(): lax.psum(jnp.sum(residual_field * smoothed, axis=(0, 1, 2)), ('gx', 'gy'))  199 us
    psum x1, blocking collectives, local(): lax.psum(jnp.sum(rounded.astype(jnp.float32) * product, axis=(0, 1, 2)),...  99.1 us
    ppermute x16, starting transfers between devices, shifted(): return lax.ppermute(value, axis, pairs)  78.1 us
    all_gather x2, blocking collectives, coarse_values(): lax.all_gather(demand, 'gx', axis=0, tiled=True)  73.5 us
    all_gather x1, blocking collectives, coarse_values(): lax.all_gather(decay, 'gx', axis=0, tiled=True)  41.5 us
    ppermute x16, waiting for transfers between devices, shifted(): return lax.ppermute(value, axis, pairs)  15.9 us
  transfers between devices with their start and end apart: 16, of which 6 were waited for; matrix products, arithmetic and copies ran while one was open for 2% of the time, Pallas kernels for 0%

commit v1 on v0

v1 whole, which is shorter than its diff:
```python
import functools

import jax
import jax.numpy as jnp
from jax import lax
from jax.experimental import pallas as pl
from jax.experimental.pallas import tpu as pltpu
from jax.sharding import PartitionSpec as P

MESH = pl.DeviceIdType.MESH
F32 = jnp.float32
BF16 = jnp.bfloat16
SX, SY, FACE, CASES = 2, 4, 64, 256
LANES = 128


def kernel(
    ny, nz, ng,
    load_hbm, schur_hbm, inverse_hbm, order_hbm, weight_hbm, decay_hbm,
    s_out, t_out, coef_out,
    load, blocks_s, blocks_p, order, weight, decay,
    wcol, edge_w, north_w, acc_e, acc_n, send_e, send_n, recv_e, recv_n, q_field,
    dk, zbuf, climb_l, trans, fg, ybuf, line_in, settled_grp, settled, ghost_col,
    mom, abuf, reduced,
    in_sem, send_sem, recv_sem,
):
    gx, gy = lax.axis_index("gx"), lax.axis_index("gy")
    nx = ny * nz
    y, z = gx // nz, gx % nz
    z_peers = [(y * nz + (z + j) % nz, gy) for j in range(1, nz)]
    y_peers = [(((y + j) % ny) * nz + z, gy) for j in range(1, ny)]
    g_peers = [(gx, (gy + j) % ng) for j in range(1, ng)]
    east, west = ((gx + 1) % nx, gy), ((gx + nx - 1) % nx, gy)
    north, south = (gx, (gy + 1) % ng), (gx, (gy + ng - 1) % ng)

    barrier = pltpu.get_barrier_semaphore()
    greeted = z_peers + y_peers + g_peers + [east, west]
    for peer in greeted:
        pl.semaphore_signal(barrier, inc=1, device_id=peer, device_id_type=MESH)

    def fetch(k, src, dst):
        copy = pltpu.make_async_copy(src, dst, in_sem.at[k])
        copy.start()
        return copy

    load_in = fetch(0, load_hbm, load)
    small_in = [fetch(1, order_hbm, order), fetch(2, weight_hbm, weight), fetch(3, decay_hbm, decay)]
    inverse_in = fetch(4, inverse_hbm, blocks_p)
    schur_in = fetch(5, schur_hbm, blocks_s)

    sent = []

    def send(src, dst, peer):
        k = len(sent)
        copy = pltpu.make_async_remote_copy(
            src_ref=src, dst_ref=dst, send_sem=send_sem.at[k], recv_sem=recv_sem.at[k],
            device_id=peer, device_id_type=MESH,
        )
        copy.start()
        sent.append(copy)
        return copy

    def arrived(copies):
        for copy in copies:
            copy.wait_recv()

    east_open = (gx < nx - 1).astype(F32)
    west_open = (gx > 0).astype(F32)
    north_open = (gy < ng - 1).astype(F32)
    south_open = (gy > 0).astype(F32)

    load_in.wait()
    for b in range(SY):
        face = load[1, b, :FACE] * east_open
        load[1, b, :FACE] = face
        edge_w[0, 2, b] = face.astype(BF16)
    for a in range(SX):
        face = load[a, SY - 1, FACE:] * north_open
        load[a, SY - 1, FACE:] = face
        north_w[0, a, SY] = face.astype(BF16)
    pl.semaphore_wait(barrier, len(greeted))
    halo = [
        send(edge_w.at[0, 2], edge_w.at[0, 0], east),
        send(north_w.at[0, :, SY], north_w.at[0, :, 0], north),
    ]

    for copy in small_in:
        copy.wait()
    wcol[...] = jnp.transpose(jnp.broadcast_to(weight[...], (LANES, 2 * FACE)))

    def demand_tiles(field):
        for a in range(SX):
            for b in range(SY):
                for h in range(2):
                    lanes = slice(h * LANES, (h + 1) * LANES)
                    value = field[a, b, :, lanes] * wcol[...]
                    dk[a, 2 * b + h : 2 * b + h + 1] = jnp.sum(value, axis=0, keepdims=True)

    demand_tiles(load)
    keep = jnp.exp(-decay[...])
    for a in range(SX):
        for b in range(SY):
            dk[SX + a, 2 * b : 2 * b + 2] = jnp.broadcast_to(keep[a : a + 1, b : b + 1], (2, LANES))
    zbuf[0, z] = dk[...]
    gather_z = [send(dk, zbuf.at[0, z], peer) for peer in z_peers]

    for b in range(SY):
        edge_w[0, 1, b] = load[0, b, :FACE].astype(BF16)
    for a in range(SX):
        for b in range(SY - 1):
            north_w[0, a, b + 1] = load[a, b, FACE:].astype(BF16)

    def fold_order(blocks):
        row = lax.broadcasted_iota(jnp.int32, (2 * FACE, 2 * FACE), 0)
        for a in range(SX):
            for b in range(SY):
                own = order[a, b]
                place = jnp.concatenate([own[0:1], own[1:2] + FACE], axis=1)
                hot_t = (row == jnp.broadcast_to(place, (2 * FACE, 2 * FACE))).astype(F32).astype(BF16)
                columns = lax.dot_general(
                    blocks[a, b, :, 2 * FACE :], hot_t, (((1,), (1,)), ((), ())), preferred_element_type=F32
                )
                blocks[a, b, :, 2 * FACE :] = columns.astype(BF16)
                rows = jnp.dot(hot_t, blocks[a, b, 2 * FACE :, :], preferred_element_type=F32)
                blocks[a, b, 2 * FACE :, :] = rows.astype(BF16)

    inverse_in.wait()
    fold_order(blocks_p)

    def group_solve(turn, first):
        group = SX * nz
        climb = jnp.zeros((8, LANES), F32)
        for r in range(group):
            k = zbuf[0, r // SX, SX + r % SX]
            climb = k * climb + zbuf[turn, r // SX, r % SX]
            climb_l[r] = climb
        back = jnp.zeros((8, LANES), F32)
        for r in range(group - 1, -1, -1):
            back = zbuf[0, r // SX, SX + r % SX] * (back + climb_l[r])
        fg[turn, 0] = climb
        fg[turn, 1] = back
        if first:
            product = jnp.ones((8, LANES), F32)
            squares = jnp.zeros((8, LANES), F32)
            for r in range(group):
                product = product * zbuf[0, r // SX, SX + r % SX]
                trans[r] = product
                squares = squares + product * product
            fg[turn, 2] = product
            fg[turn, 3] = squares
        ybuf[turn, y] = fg[turn]
        if first:
            return [send(fg.at[turn], ybuf.at[turn, y], peer) for peer in y_peers]
        return [send(fg.at[turn, 0:2], ybuf.at[turn, y, 0:2], peer) for peer in y_peers]

    def line_finish(turn):
        group = SX * nz
        climb_in = jnp.zeros((8, LANES), F32)
        for j in range(ny):
            line_in[0, j] = climb_in
            climb_in = ybuf[0, j, 2] * climb_in + ybuf[turn, j, 0]
        back = jnp.zeros((8, LANES), F32)
        for j in range(ny - 1, -1, -1):
            line_in[1, j] = back
            back = ybuf[0, j, 2] * back + ybuf[turn, j, 1] + ybuf[0, j, 3] * line_in[0, j]
            line_in[2, j] = back
        climb_in = line_in[0, y]
        back = line_in[1, y]
        for r in range(group - 1, -1, -1):
            total = climb_l[r] + trans[r] * climb_in + back
            settled_grp[r + 1] = total
            back = zbuf[0, r // SX, SX + r % SX] * total
        settled_grp[0] = climb_in + line_in[2, y]
        for r in range(SX + 1):
            settled[turn, r] = settled_grp[SX * z + r]
        return [send(settled.at[turn, 1:3], ghost_col.at[turn], north)]

    def multiply(blocks, now, turn):
        total = jnp.zeros((8, CASES), F32)
        copies = []
        for a in (1, 0):
            for b in range(SY):
                field = jnp.concatenate(
                    [edge_w[now, a + 1, b], north_w[now, a, b + 1], edge_w[now, a, b], north_w[now, a, b]], axis=0
                )
                image = jnp.dot(blocks[a, b], field, preferred_element_type=F32)
                total = total + jnp.sum(
                    (image * field.astype(F32)).reshape(2 * FACE * 2 // 8, 8, CASES), axis=0
                )
                img_e, img_n = image[:FACE], image[FACE : 2 * FACE]
                img_w, img_s = image[2 * FACE : 3 * FACE], image[3 * FACE :]
                if a == 1:
                    acc_e[2, b] = img_e
                    send_e[turn, 0, b] = img_e.astype(BF16)
                    acc_e[1, b] = img_w
                else:
                    acc_e[1, b] = acc_e[1, b] + img_e
                    acc_e[0, b] = img_w
                    send_e[turn, 1, b] = img_w.astype(BF16)
                acc_n[a, b + 1] = img_n
                if b == 0:
                    acc_n[a, 0] = img_s
                    send_n[turn, 1, a] = img_s.astype(BF16)
                else:
                    acc_n[a, b] = acc_n[a, b] + img_s
                if b == SY - 1:
                    send_n[turn, 0, a] = img_n.astype(BF16)
            if turn < 3:
                if a == 1:
                    copies.append(send(send_e.at[turn, 0], recv_e.at[turn, 0], east))
                else:
                    copies.append(send(send_e.at[turn, 1], recv_e.at[turn, 1], west))
        if turn < 3:
            copies.append(send(send_n.at[turn, 0], recv_n.at[turn, 0], north))
            copies.append(send(send_n.at[turn, 1], recv_n.at[turn, 1], south))
        return total, copies

    def edge_sum(turn, r, b):
        if r == 0:
            return (acc_e[0, b] + recv_e[turn, 0, b].astype(F32)) * west_open
        if r == SX:
            return (acc_e[2, b] + recv_e[turn, 1, b].astype(F32)) * east_open
        return acc_e[r, b]

    def north_sum(turn, a, c):
        if c == 0:
            return (acc_n[a, 0] + recv_n[turn, 0, a].astype(F32)) * south_open
        if c == SY:
            return (acc_n[a, SY] + recv_n[turn, 1, a].astype(F32)) * north_open
        return acc_n[a, c]

    def smooth(turn, coarse, now, out):
        def coarse_part(rows, tile):
            return jnp.concatenate(
                [wcol[rows] * tile[0:1], wcol[rows] * tile[1:2]], axis=1
            )

        for r in range(SX + 1):
            for b in range(SY):
                value = coarse_part(slice(0, FACE), settled[coarse, r, 2 * b : 2 * b + 2])
                if r == 0:
                    value = value * west_open
                if r == SX:
                    value = value * east_open
                value = value + 0.25 * edge_sum(turn, r, b)
                edge_w[now, r, b] = value.astype(BF16)
                if r > 0:
                    out[r - 1, b, :FACE] = value
        for a in range(SX):
            for c in range(SY + 1):
                if c == 0:
                    value = coarse_part(slice(FACE, 2 * FACE), ghost_col[coarse, a, 6:8]) * south_open
                else:
                    value = coarse_part(slice(FACE, 2 * FACE), settled[coarse, a + 1, 2 * c - 2 : 2 * c])
                if c == SY:
                    value = value * north_open
                value = value + 0.25 * north_sum(turn, a, c)
                north_w[now, a, c] = value.astype(BF16)
                if c > 0:
                    out[a, c - 1, FACE:] = value

    def dot(left, right):
        total = jnp.zeros((8, CASES), F32)
        for a in range(SX):
            for b in range(SY):
                total = total + jnp.sum((left[a, b] * right[a, b]).reshape(2 * FACE // 8, 8, CASES), axis=0)
        return total

    arrived(gather_z)
    gather_y = group_solve(0, True)
    arrived(halo)
    _, halo = multiply(blocks_p, 0, 0)
    schur_in.wait()
    fold_order(blocks_s)
    arrived(gather_y)
    column = line_finish(0)
    arrived(halo)
    arrived(column)
    smooth(0, 0, 1, s_out)

    moment1, halo = multiply(blocks_s, 1, 1)
    moment0 = dot(load, s_out)
    arrived(halo)
    for r in range(SX + 1):
        for b in range(SY):
            value = edge_sum(1, r, b)
            edge_w[2, r, b] = value.astype(BF16)
            if r > 0:
                q_field[r - 1, b, :FACE] = value
    for a in range(SX):
        for c in range(SY + 1):
            value = north_sum(1, a, c)
            north_w[2, a, c] = value.astype(BF16)
            if c > 0:
                q_field[a, c - 1, FACE:] = value
    for copy in gather_z:
        copy.wait_send()
    demand_tiles(q_field)
    zbuf[1, z] = dk[...]
    gather_z2 = [send(dk.at[0:2], zbuf.at[1, z, 0:2], peer) for peer in z_peers]
    _, halo = multiply(blocks_p, 2, 2)
    arrived(gather_z2)
    gather_y2 = group_solve(1, False)
    arrived(gather_y2)
    column = line_finish(1)
    arrived(halo)
    arrived(column)
    smooth(2, 1, 3, t_out)
    moment3, _ = multiply(blocks_s, 3, 3)
    moment2 = dot(q_field, t_out)

    for m, value in enumerate((moment0, moment1, moment2, moment3)):
        whole = jnp.sum(value, axis=0, keepdims=True)
        for h in range(2):
            mom[0, 2 * m + h : 2 * m + h + 1] = whole[:, h * LANES : (h + 1) * LANES]

    for stage, (peers, count, me) in enumerate(((g_peers, ng, gy), (z_peers, nz, z), (y_peers, ny, y))):
        abuf[stage, me] = mom[stage]
        copies = [send(mom.at[stage], abuf.at[stage, me], peer) for peer in peers]
        arrived(copies)
        value = abuf[stage, 0]
        for j in range(1, count):
            value = value + abuf[stage, j]
        if stage < 2:
            mom[stage + 1] = value
        else:
            reduced[...] = value

    m0, m1, m2, m3 = (reduced[2 * m : 2 * m + 2] for m in range(4))
    step0 = m0 / m1
    inner1 = step0 * step0 * m2 - m0
    beta = inner1 / m0
    mixed = m1 - step0 * m2
    curvature1 = mixed - step0 * m2 + step0 * step0 * m3 + 2.0 * beta * mixed + beta * beta * m1
    step1 = inner1 / curvature1
    coef_out[0:2] = step0 + step1 * (1.0 + beta)
    coef_out[2:4] = -step0 * step1

    waited = set(id(copy) for copy in gather_z)
    for copy in sent:
        if id(copy) not in waited:
            copy.wait_send()


def local(mesh_sizes, load_field, schur_blocks, local_inverse, face_order, coarse_weights, coarse_decay):
    ny, nz, ng = mesh_sizes
    big = max(ny, nz, ng)
    n_sends = 2 + 3 * 4 + 2 * (nz - 1 + ny - 1) + 2 + (ng - 1 + nz - 1 + ny - 1)
    field = (SX, SY, 2 * FACE, CASES)
    vmem = pl.BlockSpec(memory_space=pltpu.VMEM)
    s_field, t_field, coef = pl.pallas_call(
        functools.partial(kernel, ny, nz, ng),
        out_shape=[
            jax.ShapeDtypeStruct(field, F32),
            jax.ShapeDtypeStruct(field, F32),
            jax.ShapeDtypeStruct((4, LANES), F32),
        ],
        in_specs=[pl.BlockSpec(memory_space=pl.ANY)] * 6,
        out_specs=[vmem] * 3,
        scratch_shapes=[
            pltpu.VMEM(field, F32),
            pltpu.VMEM((SX, SY, 4 * FACE, 4 * FACE), BF16),
            pltpu.VMEM((SX, SY, 4 * FACE, 4 * FACE), BF16),
            pltpu.VMEM((SX, SY, 2, FACE), jnp.int32),
            pltpu.VMEM((1, 2 * FACE), F32),
            pltpu.VMEM((SX, SY), F32),
            pltpu.VMEM((2 * FACE, LANES), F32),
            pltpu.VMEM((4, SX + 1, SY, FACE, CASES), BF16),
            pltpu.VMEM((4, SX, SY + 1, FACE, CASES), BF16),
            pltpu.VMEM((SX + 1, SY, FACE, CASES), F32),
            pltpu.VMEM((SX, SY + 1, FACE, CASES), F32),
            pltpu.VMEM((4, 2, SY, FACE, CASES), BF16),
            pltpu.VMEM((4, 2, SX, FACE, CASES), BF16),
            pltpu.VMEM((3, 2, SY, FACE, CASES), BF16),
            pltpu.VMEM((3, 2, SX, FACE, CASES), BF16),
            pltpu.VMEM(field, F32),
            pltpu.VMEM((2 * SX, 8, LANES), F32),
            pltpu.VMEM((2, nz, 2 * SX, 8, LANES), F32),
            pltpu.VMEM((SX * nz, 8, LANES), F32),
            pltpu.VMEM((SX * nz, 8, LANES), F32),
            pltpu.VMEM((2, 4, 8, LANES), F32),
            pltpu.VMEM((2, ny, 4, 8, LANES), F32),
            pltpu.VMEM((3, ny, 8, LANES), F32),
            pltpu.VMEM((SX * nz + 1, 8, LANES), F32),
            pltpu.VMEM((2, SX + 1, 8, LANES), F32),
            pltpu.VMEM((2, SX, 8, LANES), F32),
            pltpu.VMEM((3, 8, LANES), F32),
            pltpu.VMEM((3, big, 8, LANES), F32),
            pltpu.VMEM((8, LANES), F32),
            pltpu.SemaphoreType.DMA((6,)),
            pltpu.SemaphoreType.DMA((n_sends,)),
            pltpu.SemaphoreType.DMA((n_sends,)),
        ],
        compiler_params=pltpu.CompilerParams(
            collective_id=0, has_side_effects=True, vmem_limit_bytes=40 << 20
        ),
        cost_estimate=pl.CostEstimate(flops=1_100_000_000, bytes_accessed=6 << 20, transcendentals=8),
    )(load_field, schur_blocks, local_inverse, face_order, coarse_weights.reshape(1, -1), coarse_decay)
    first, second = coef[0:2].reshape(CASES), coef[2:4].reshape(CASES)
    return first * s_field + second * t_field


def solution(mesh):
    nx, ng = mesh.shape["gx"], mesh.shape["gy"]
    nz = 8 if nx % 8 == 0 else 2
    in_specs = (
        P("gx", "gy", None, None),
        P("gx", "gy", None, None),
        P("gx", "gy", None, None),
        P("gx", "gy", None, None),
        P(),
        P("gx", "gy"),
    )
    return jax.shard_map(
        functools.partial(local, (nx // nz, nz, ng)),
        mesh=mesh, in_specs=in_specs, out_specs=P("gx", "gy", None, None), check_vma=False,
    )
```

time: 539 us -> 68.4 us (0.13)
  blocking collectives: 413 us -> 0 us
  starting transfers between devices: 78.1 us -> 0 us
  Pallas kernels: 0 us -> 61.9 us
  waiting for transfers between devices: 15.9 us -> 0 us
  matrix products: 14 us -> 0 us
  other arithmetic: 12.1 us -> 1.14 us
    psum x3 -> x0, blocking collectives: 298 us -> none  [the longest x2 199 us: global_inner(): lax.psum(jnp.sum(residual_field * smoothed, axis=(0, 1, 2)), ('gx', 'gy'))]
    all_gather x3 -> x0, blocking collectives: 115 us -> none  [the longest x2 73.5 us: coarse_values(): lax.all_gather(demand, 'gx', axis=0, tiled=True)]
    ppermute x16 -> x0, starting transfers between devices: 78.1 us -> none  [shifted(): return lax.ppermute(value, axis, pairs)]
    pallas_call x0 -> x1, Pallas kernels: none -> 61.9 us  [local(): pl.pallas_call(functools.partial(kernel, ny, nz, ng), out_shape=[jax.Shap...]
    ppermute x16 -> x0, waiting for transfers between devices: 15.9 us -> none  [shifted(): return lax.ppermute(value, axis, pairs)]
    dot_general x26 -> x0, matrix products: 14 us -> none  [the longest x2 2.1 us: line_solve(): jnp.einsum('tay,tyr->ayr', transfer, climbed, precision=lax.Precision.HIG...]
  transfers between devices with their start and end apart: 16 -> 0, of which waited for: 6 -> 0; matrix products, arithmetic and copies ran while one was open for 2% -> 0% of each run, Pallas kernels for 0% -> 0%
where the time goes in v1:
time: 68.4 us; the launch traced here: 68.1 us
  Pallas kernels  61.9 us (90%)
  local copies, waits for them, and re-layouts  5.05 us (7%)
  other arithmetic  1.14 us (2%)
    pallas_call x1, Pallas kernels, local(): pl.pallas_call(functools.partial(kernel, ny, nz, ng), out_shape=[jax.Shap...  61.9 us
    unnamed x12, local copies, waits for them, and re-layouts  5.05 us

profile of v1, /device:TPU:1, one launch (start us, length us, event | category | flops | bytes accessed | tf_op | source)
XLA Modules:
  0.0 68.1 jit_solution(14323116311191960189)
XLA Ops:
  0.0 0.0 copy-start.4
  0.0 0.0 copy-start.5
  0.0 0.7 copy-done.4
  0.7 0.0 copy-done.5
  0.7 0.0 copy-start
  0.7 1.2 %copy-done = f32[2,4,128,256]{3,2,1,0:T(8,128)S(1)} copy-done((f32[2,4,128,256]{3,2,1,0:T(8,128)S(1)}, f32[2,4,128,256]{3,2,1,0:T(8,128)}, u32[]{:S(2)}) %copy-start) | copy-done | bytes 1048600
  1.9 0.0 copy-start.1
  1.9 1.2 %copy-done.1 = bf16[2,4,256,256]{3,2,1,0:T(8,128)(2,1)S(1)} copy-done((bf16[2,4,256,256]{3,2,1,0:T(8,128)(2,1)S(1)}, bf16[2,4,256,256]{3,2,1,0:T(8,128)(2,1)}, u32[]{:S(2)}) %copy-start.1) | copy-done | bytes 1048600
  3.1 0.0 copy-start.2
  3.1 1.2 %copy-done.2 = bf16[2,4,256,256]{3,2,1,0:T(8,128)(2,1)S(1)} copy-done((bf16[2,4,256,256]{3,2,1,0:T(8,128)(2,1)S(1)}, bf16[2,4,256,256]{3,2,1,0:T(8,128)(2,1)}, u32[]{:S(2)}) %copy-start.2) | copy-done | bytes 1048600
  4.4 0.0 copy-start.3
  4.4 0.7 %copy-done.3 = s32[2,4,2,64]{3,2,1,0:T(2,128)S(1)} copy-done((s32[2,4,2,64]{3,2,1,0:T(2,128)S(1)}, s32[2,4,2,64]{3,2,1,0:T(2,128)}, u32[]{:S(2)}) %copy-start.3) | copy-done | bytes 4120
  5.1 61.9 %shard_map.64 = (f32[2,4,128,256]{3,2,1,0:T(8,128)S(1)}, f32[2,4,128,256]{3,2,1,0:T(8,128)S(1)}, f32[4,128]{1,0:T(4,128)S(1)}) custom-call(f32[2,4,128,256]{3,2,1,0:T(8,128)S(1)} %copy-done, bf16[2,4,256,256]{3,2,1,0:T(8,128)(2,1)S(1)} %copy-done.1, bf16[2,4,256,256]{3,2,1,0:T(8,128)(2,1)S(1)} %copy-done.2, s32[2,4,2,64]{3,2,1,0:T(2,128)S(1)} %copy-done.3, ...), custom_call_target="tpu_custom_call" | custom-call | flops 1100000000 | bytes 6291456 | tf_op jit(solution)/shard_map/pallas_call | solution.py:351
  67.0 1.1 %multiply_add_fusion = f32[2,4,128,256]{3,2,1,0:T(8,128)} fusion(f32[2,4,128,256]{3,2,1,0:T(8,128)S(1)} %get-tuple-element.10, f32[2,4,128,256]{3,2,1,0:T(8,128)S(1)} %get-tuple-element.9, f32[256]{0:T(256)S(1)} %get-tuple-element.12, f32[256]{0:T(256)S(1)} %get-tuple-element.11), kind=kLoop, calls=%fused_computation | loop fusion | flops 786432 | bytes 3147776 | tf_op jit(solution)/shard_map/add | solution.py:400
  (1 shorter events, 0.0 us)
Async XLA Ops:
  0.0 0.7 copy-start.4
  0.0 0.7 copy-start.5
  0.7 1.2 %copy-start = (f32[2,4,128,256]{3,2,1,0:T(8,128)S(1)}, f32[2,4,128,256]{3,2,1,0:T(8,128)}, u32[]{:S(2)}) copy-start(f32[2,4,128,256]{3,2,1,0:T(8,128)} %load_hbm.1) | copy-start | bytes 3145732
  1.9 1.2 %copy-start.1 = (bf16[2,4,256,256]{3,2,1,0:T(8,128)(2,1)S(1)}, bf16[2,4,256,256]{3,2,1,0:T(8,128)(2,1)}, u32[]{:S(2)}) copy-start(bf16[2,4,256,256]{3,2,1,0:T(8,128)(2,1)} %schur_hbm.1) | copy-start | bytes 3145732
  3.1 1.2 %copy-start.2 = (bf16[2,4,256,256]{3,2,1,0:T(8,128)(2,1)S(1)}, bf16[2,4,256,256]{3,2,1,0:T(8,128)(2,1)}, u32[]{:S(2)}) copy-start(bf16[2,4,256,256]{3,2,1,0:T(8,128)(2,1)} %inverse_hbm.1) | copy-start | bytes 3145732
  4.4 0.7 %copy-start.3 = (s32[2,4,2,64]{3,2,1,0:T(2,128)S(1)}, s32[2,4,2,64]{3,2,1,0:T(2,128)}, u32[]{:S(2)}) copy-start(s32[2,4,2,64]{3,2,1,0:T(2,128)} %order_hbm.1) | copy-start | bytes 12292

commit v2 on v1

v2 whole, which is shorter than its diff:
```python
import functools

import jax
import jax.numpy as jnp
from jax import lax
from jax.experimental import pallas as pl
from jax.experimental.pallas import tpu as pltpu
from jax.sharding import PartitionSpec as P

MESH = pl.DeviceIdType.MESH
F32 = jnp.float32
BF16 = jnp.bfloat16
SX, SY, FACE, CASES = 2, 4, 64, 256
LANES = 128
TILE = 8
ORDER = (3, 2, 1, 0)
PLACE0, PLACE1 = 0, 0
CUT = 1


def kernel(
    ny, nz, ng,
    load_hbm, schur_hbm, inverse_hbm, order_hbm, weight_hbm, decay_hbm,
    s_hbm, t_hbm, coef_out,
    s_out, t_out, load, blocks_s, blocks_p, order, weight, decay,
    wcol, edge_w, north_w, acc_e, acc_n, send_e, send_n, recv_e, recv_n,
    ksrc, kz, kw, ykw, zsrc, za, zs, south_part, d_all, k_all, climb_l, trans, fg, ybuf, line_in,
    settled_grp, settled, ghost_col,
    mom, mid, sum_a, sum_b, mom3, mid3, sum3_a, sum3_b,
    in_sem, send_sem, recv_sem,
):
    gx, gy = lax.axis_index("gx"), lax.axis_index("gy")
    nx, nc, group = ny * nz, ng // 2, SX * nz
    y, z, x, core = gx // nz, gx % nz, gy // 2, gy % 2
    east, west = ((gx + 1) % nx, gy), ((gx + nx - 1) % nx, gy)
    north, south = (gx, (gy + 1) % ng), (gx, (gy + ng - 1) % ng)

    def ring(j):
        return y * nz + (z + j) % nz

    z_peers = [(ring(j), gy) for j in range(1, nz)]
    y_peers = [(((y + j) % ny) * nz + z, gy) for j in range(1, ny)]
    zn_peers = [(ring(j), (gy + 1) % ng) for j in range(nz)]
    zs_peers = [(ring(j), (gy + ng - 1) % ng) for j in range(nz)]
    a_peers = z_peers + [(ring(j), 2 * x + (1 - core)) for j in range(nz)]
    b_peers = [
        (((y + j) % ny) * nz + z, 2 * ((x + i) % nc) + core) for j in range(ny) for i in range(nc) if i + j
    ]

    barrier = pltpu.get_barrier_semaphore()
    greeted = [east, west, north, south] + zn_peers + zs_peers + a_peers + b_peers
    for peer in greeted:
        pl.semaphore_signal(barrier, inc=1, device_id=peer, device_id_type=MESH)

    fetched = []

    def fetch(src, dst):
        copy = pltpu.make_async_copy(src, dst, in_sem.at[len(fetched)])
        copy.start()
        fetched.append(copy)
        return copy

    decay_in = fetch(decay_hbm, decay)
    load_cut = [
        fetch(load_hbm.at[1, :, :FACE], load.at[1, :, :FACE]),
        fetch(load_hbm.at[:, SY - 1, FACE:], load.at[:, SY - 1, FACE:]),
    ]
    small_in = [fetch(order_hbm, order), fetch(weight_hbm, weight)]
    load_rest = [
        fetch(load_hbm.at[0, :, :FACE], load.at[0, :, :FACE]),
        fetch(load_hbm.at[:, : SY - 1, FACE:], load.at[:, : SY - 1, FACE:]),
    ]
    inverse_in = fetch(inverse_hbm, blocks_p)
    schur_in = fetch(schur_hbm, blocks_s)

    sent = []

    def send(src, dst, peer):
        k = len(sent)
        copy = pltpu.make_async_remote_copy(
            src_ref=src, dst_ref=dst, send_sem=send_sem.at[k], recv_sem=recv_sem.at[k],
            device_id=peer, device_id_type=MESH,
        )
        copy.start()
        sent.append(copy)
        return copy

    def arrived(copies):
        for copy in copies:
            copy.wait_recv()

    east_open = (gx < nx - 1).astype(F32)
    west_open = (gx > 0).astype(F32)
    north_open = (gy < ng - 1).astype(F32)
    south_open = (gy > 0).astype(F32)

    decay_in.wait()
    ksrc[...] = jnp.zeros((SX, LANES), F32)
    ksrc[:, 0:SY] = jnp.exp(-decay[...])
    kz[z] = ksrc[...]
    for copy in load_cut:
        copy.wait()
    for b in range(SY):
        face = load[1, b, :FACE] * east_open
        load[1, b, :FACE] = face
        edge_w[0, 2, b] = face.astype(BF16)
    for a in range(SX):
        face = load[a, SY - 1, FACE:] * north_open
        load[a, SY - 1, FACE:] = face
        north_w[0, a, SY] = face.astype(BF16)
    pl.semaphore_wait(barrier, len(greeted))
    gather_k = [send(ksrc, kz.at[z], peer) for peer in z_peers]
    halo_n = [send(north_w.at[0, :, SY], north_w.at[0, :, 0], north)]
    halo_e = {
        b + CUT - 1: [send(edge_w.at[0, 2, b : b + CUT], edge_w.at[0, 0, b : b + CUT], east)]
        for b in range(SY - CUT, -1, -CUT)
    }

    for copy in small_in + load_rest:
        copy.wait()
    wcol[...] = jnp.transpose(jnp.broadcast_to(weight[...], (LANES, 2 * FACE)))
    w_east, w_north = wcol[:FACE], wcol[FACE:]

    def weigh(face, weights):
        value = [jnp.sum(face[:, h * LANES : (h + 1) * LANES] * weights, axis=0, keepdims=True) for h in range(2)]
        return jnp.concatenate(value, axis=0)

    def gather_ring(turn, rows):
        za[turn, z, 0:rows] = zsrc[turn, 0:rows]
        copies = []
        if turn:
            copies += [send(south_part, zs.at[z], peer) for peer in zs_peers]
        copies += [send(zsrc.at[turn, 0:rows], za.at[turn, z, 0:rows], peer) for peer in z_peers]
        return copies

    for a in range(SX):
        for b in range(SY):
            rows = slice(2 * b, 2 * b + 2)
            zsrc[0, a, rows] = weigh(load[a, b, :FACE], w_east) + weigh(load[a, b, FACE:], w_north)
    gather_z = gather_ring(0, SX)

    for b in range(SY):
        edge_w[0, 1, b] = load[0, b, :FACE].astype(BF16)
    for a in range(SX):
        for b in range(SY - 1):
            north_w[0, a, b + 1] = load[a, b, FACE:].astype(BF16)

    def fold_order(blocks):
        row = lax.broadcasted_iota(jnp.int32, (2 * FACE, 2 * FACE), 0)
        for a in range(SX):
            for b in range(SY):
                own = order[a, b]
                place = jnp.concatenate([own[0:1], own[1:2] + FACE], axis=1)
                hot_t = (row == jnp.broadcast_to(place, (2 * FACE, 2 * FACE))).astype(F32).astype(BF16)
                columns = lax.dot_general(
                    blocks[a, b, :, 2 * FACE :], hot_t, (((1,), (1,)), ((), ())), preferred_element_type=F32
                )
                blocks[a, b, :, 2 * FACE :] = columns.astype(BF16)
                rows = jnp.dot(hot_t, blocks[a, b, 2 * FACE :, :], preferred_element_type=F32)
                blocks[a, b, 2 * FACE :, :] = rows.astype(BF16)

    inverse_in.wait()
    fold_order(blocks_p)

    def group_keep():
        for r in range(group):
            for b in range(SY):
                rate = kz[r // SX, r % SX : r % SX + 1, b : b + 1]
                k_all[r, 2 * b : 2 * b + 2] = jnp.broadcast_to(rate, (2, LANES))
        product = jnp.ones((TILE, LANES), F32)
        squares = jnp.zeros((TILE, LANES), F32)
        for r in range(group):
            product = product * k_all[r]
            trans[r] = product
            squares = squares + product * product
        kw[0] = product
        kw[1] = squares
        ykw[y] = kw[...]
        return [send(kw, ykw.at[y], peer) for peer in y_peers]

    def group_solve(turn):
        for r in range(group):
            s, a = r // SX, r % SX
            if turn == 0:
                d_all[turn, r] = za[0, s, a]
            else:
                own = za[1, s, a + 1]
                if a == SX - 1 and s + 1 < nz:
                    own = own + za[1, s + 1, 0]
                d_all[turn, r] = own
                d_all[turn, r, 6:8] = d_all[turn, r, 6:8] + zs[s, a]
        climb = jnp.zeros((TILE, LANES), F32)
        for r in range(group):
            climb = k_all[r] * climb + d_all[turn, r]
            climb_l[turn, r] = climb
        back = jnp.zeros((TILE, LANES), F32)
        for r in range(group - 1, -1, -1):
            back = k_all[r] * (back + climb_l[turn, r])
        fg[turn, 0] = climb
        fg[turn, 1] = back
        if turn:
            fg[turn, 2] = za[1, 0, 0]
        count = 2 + turn
        ybuf[turn, y, 0:count] = fg[turn, 0:count]
        return [send(fg.at[turn, 0:count], ybuf.at[turn, y, 0:count], peer) for peer in y_peers]

    pending = {}

    def line_finish(turn):
        climb_in = jnp.zeros((TILE, LANES), F32)
        for j in range(ny):
            line_in[0, j] = climb_in
            climb_in = ykw[j, 0] * climb_in + ybuf[turn, j, 0]
            if turn:
                climb_in = climb_in + ybuf[1, (j + 1) % ny, 2]
        back = jnp.zeros((TILE, LANES), F32)
        for j in range(ny - 1, -1, -1):
            line_in[1, j] = back
            if turn:
                back = back + ybuf[1, (j + 1) % ny, 2]
            back = ykw[j, 0] * back + ybuf[turn, j, 1] + ykw[j, 1] * line_in[0, j]
            line_in[2, j] = back
        climb_in = line_in[0, y]
        back = line_in[1, y]
        if turn:
            handed = ybuf[1, (y + 1) % ny, 2]
            back = back + handed
            d_all[turn, group - 1] = d_all[turn, group - 1] + handed
        for r in range(group - 1, -1, -1):
            total = climb_l[turn, r] + trans[r] * climb_in + back
            settled_grp[turn, r + 1] = total
            back = k_all[r] * total
        settled_grp[turn, 0] = climb_in + line_in[2, y]
        total = jnp.zeros((8, LANES), F32)
        for r in range(SX + 1):
            value = settled_grp[turn, SX * z + r]
            settled[turn, r] = value
            if r == SX:
                pending["column"] = [send(settled.at[turn, 1:3, 6:8], ghost_col.at[turn], north)]
            if r:
                total = total + value[0:8] * d_all[turn, SX * z + r - 1, 0:8]
        return total[0:2] + total[2:4] + total[4:6] + total[6:8]

    def edge_sum(turn, r, b):
        if r == 0:
            return (acc_e[turn % 2, 0, b] + recv_e[turn, 0, b].astype(F32)) * west_open
        if r == SX:
            return (acc_e[turn % 2, 2, b] + recv_e[turn, 1, b].astype(F32)) * east_open
        return acc_e[turn % 2, r, b]

    def north_sum(turn, a, c):
        if c == 0:
            return (acc_n[turn % 2, a, 0] + recv_n[turn, 0, a].astype(F32)) * south_open
        if c == SY:
            return (acc_n[turn % 2, a, SY] + recv_n[turn, 1, a].astype(F32)) * north_open
        return acc_n[turn % 2, a, c]

    def spread(weights, pair):
        return jnp.concatenate([weights * pair[0:1], weights * pair[1:2]], axis=1)

    def edge_face(turn, coarse, out, r, b):
        value = edge_sum(turn, r, b)
        if coarse is not None:
            part = spread(w_east, settled[coarse, r, 2 * b : 2 * b + 2])
            if r == 0:
                part = part * west_open
            if r == SX:
                part = part * east_open
            value = 0.25 * value + part
            if r > 0:
                out[r - 1, b, :FACE] = value
        edge_w[turn + 1, r, b] = value.astype(BF16)

    def north_face(turn, coarse, out, a, c):
        value = north_sum(turn, a, c)
        if coarse is not None:
            pair = settled[coarse, a + 1, 2 * c - 2 : 2 * c] if c else ghost_col[coarse, a]
            part = spread(w_north, pair)
            if c == 0:
                part = part * south_open
            if c == SY:
                part = part * north_open
            value = 0.25 * value + part
            if c > 0:
                out[a, c - 1, FACE:] = value
        north_w[turn + 1, a, c] = value.astype(BF16)

    def stage(turn, blocks, halo_e, halo_n, coarse=None, out=None, between=None):
        if turn > 0:
            for b in range(SY):
                edge_face(turn - 1, coarse, out, 1, b)
            for a in range(SX):
                for c in range(1, SY):
                    north_face(turn - 1, coarse, out, a, c)
        now = turn % 2
        total = jnp.zeros((8, CASES), F32)
        next_e, next_n = {}, []
        for place, b in enumerate(ORDER):
            if between is not None and place == between[0]:
                between[1]()
            if turn == 0:
                if b == 0:
                    arrived(halo_n)
            elif b == SY - 1:
                arrived(halo_n[1])
                for a in range(SX):
                    north_face(turn - 1, coarse, out, a, SY)
            elif b == 0:
                arrived(halo_n[0])
                if coarse is not None:
                    arrived(pending["column"])
                for a in range(SX):
                    north_face(turn - 1, coarse, out, a, 0)
            if b in halo_e:
                arrived(halo_e[b])
            if turn > 0:
                edge_face(turn - 1, coarse, out, 2, b)
                edge_face(turn - 1, coarse, out, 0, b)
            for a in (1, 0):
                field = jnp.concatenate(
                    [edge_w[turn, a + 1, b], north_w[turn, a, b + 1], edge_w[turn, a, b], north_w[turn, a, b]], axis=0
                )
                image = jnp.dot(blocks[a, b], field, preferred_element_type=F32)
                total = total + jnp.sum((image * field.astype(F32)).reshape(4 * FACE // 8, 8, CASES), axis=0)
                if turn == 3:
                    continue
                img_e, img_n = image[:FACE], image[FACE : 2 * FACE]
                img_w, img_s = image[2 * FACE : 3 * FACE], image[3 * FACE :]
                if a == 1:
                    acc_e[now, 2, b] = img_e
                    send_e[turn, 0, b] = img_e.astype(BF16)
                    acc_e[now, 1, b] = img_w
                else:
                    acc_e[now, 1, b] = acc_e[now, 1, b] + img_e
                    acc_e[now, 0, b] = img_w
                    send_e[turn, 1, b] = img_w.astype(BF16)
                if b == SY - 1:
                    acc_n[now, a, b + 1] = img_n
                else:
                    acc_n[now, a, b + 1] = acc_n[now, a, b + 1] + img_n
                acc_n[now, a, b] = img_s
                if b == 0:
                    send_n[turn, 1, a] = img_s.astype(BF16)
                if b == SY - 1:
                    send_n[turn, 0, a] = img_n.astype(BF16)
            if turn == 3:
                continue
            if b % CUT == 0:
                some = slice(b, b + CUT)
                next_e[b + CUT - 1] = [
                    send(send_e.at[turn, 0, some], recv_e.at[turn, 0, some], east),
                    send(send_e.at[turn, 1, some], recv_e.at[turn, 1, some], west),
                ]
            if b == SY - 1:
                to_north = send(send_n.at[turn, 0], recv_n.at[turn, 0], north)
            if b == 0:
                to_south = send(send_n.at[turn, 1], recv_n.at[turn, 1], south)
        if turn < 3:
            next_n = [[to_north], [to_south]]
        if between is not None and between[0] == SY:
            between[1]()
        return total, next_e, next_n

    def by_half(total):
        whole = jnp.sum(total, axis=0, keepdims=True)
        return jnp.concatenate([whole[:, :LANES], whole[:, LANES:]], axis=0)

    def all_sum(source, middle, buf_a, buf_b):
        def first():
            buf_a[2 * z + core] = source[...]
            return [send(source, buf_a.at[2 * z + core], peer) for peer in a_peers]

        def second(copies):
            arrived(copies)
            value = buf_a[0]
            for k in range(1, 2 * nz):
                value = value + buf_a[k]
            middle[...] = value
            buf_b[nc * y + x] = value
            return [send(middle, buf_b.at[nc * y + x], peer) for peer in b_peers]

        def third(copies):
            arrived(copies)
            value = buf_b[0]
            for k in range(1, ny * nc):
                value = value + buf_b[k]
            return value

        return first, second, third

    def solve_ring(turn, copies):
        def run():
            if turn == 0:
                arrived(gather_k)
                pending["keep"] = group_keep()
            arrived(copies)
            pending[turn] = group_solve(turn)

        return run

    total0, halo_e, halo_n = stage(0, blocks_p, halo_e, halo_n, between=(PLACE0, solve_ring(0, gather_z)))
    schur_in.wait()
    fold_order(blocks_s)
    arrived(pending["keep"])
    arrived(pending[0])
    coarse0 = line_finish(0)
    total1, halo_e, halo_n = stage(1, blocks_s, halo_e, halo_n, 0, s_out)

    s_done = fetch(s_out, s_hbm)
    for b in range(SY):
        rows = slice(2 * b, 2 * b + 2)
        zsrc[1, 0, rows] = weigh(acc_e[1, 0, b], w_east) * west_open
        for a in range(SX):
            part_e, part_n = weigh(acc_e[1, a + 1, b], w_east), weigh(acc_n[1, a, b + 1], w_north)
            if a == SX - 1:
                part_e = part_e * east_open
            if b == SY - 1:
                part_n = part_n * north_open
            zsrc[1, a + 1, rows] = part_e + part_n
    for a in range(SX):
        south_part[a] = weigh(acc_n[1, a, 0], w_north) * south_open
    gather_z = gather_ring(1, SX + 1)

    mom[0:2] = 0.25 * by_half(total0) + coarse0
    mom[2:4] = by_half(total1)
    mom[6:8] = jnp.zeros((2, LANES), F32)

    total2, halo_e, halo_n = stage(2, blocks_p, halo_e, halo_n, between=(PLACE1, solve_ring(1, gather_z)))
    arrived(pending[1])
    coarse1 = line_finish(1)
    mom[4:6] = 0.25 * by_half(total2) + coarse1
    early = all_sum(mom, mid, sum_a, sum_b)
    early_a = early[0]()

    total3, _, _ = stage(3, blocks_s, halo_e, halo_n, 1, t_out)
    mom3[...] = by_half(total3)
    t_done = fetch(t_out, t_hbm)
    late = all_sum(mom3, mid3, sum3_a, sum3_b)
    late_a = late[0]()
    early_b = early[1](early_a)
    late_b = late[1](late_a)
    reduced = early[2](early_b)
    m3 = late[2](late_b)
    m0, m1, m2 = reduced[0:2], reduced[2:4], reduced[4:6]
    step0 = m0 / m1
    inner1 = step0 * step0 * m2 - m0
    beta = inner1 / m0
    mixed = m1 - step0 * m2
    curvature1 = mixed - step0 * m2 + step0 * step0 * m3 + 2.0 * beta * mixed + beta * beta * m1
    step1 = inner1 / curvature1
    coef_out[0:2] = step0 + step1 * (1.0 + beta)
    coef_out[2:4] = -step0 * step1

    s_done.wait()
    t_done.wait()
    for copy in sent:
        copy.wait_send()


def local(mesh_sizes, load_field, schur_blocks, local_inverse, face_order, coarse_weights, coarse_decay):
    ny, nz, ng = mesh_sizes
    nc, group = ng // 2, SX * nz
    n_sends = 1 + 3 * 2 + 7 * (SY // CUT) + 3 * (nz - 1 + ny - 1) + nz + 2 + 2 * (2 * nz - 1 + ny * nc - 1)
    field = (SX, SY, 2 * FACE, CASES)
    vmem = pl.BlockSpec(memory_space=pltpu.VMEM)
    s_field, t_field, coef = pl.pallas_call(
        functools.partial(kernel, ny, nz, ng),
        out_shape=[
            jax.ShapeDtypeStruct(field, F32),
            jax.ShapeDtypeStruct(field, F32),
            jax.ShapeDtypeStruct((4, LANES), F32),
        ],
        in_specs=[pl.BlockSpec(memory_space=pltpu.HBM)] * 6,
        out_specs=[pl.BlockSpec(memory_space=pltpu.HBM)] * 2 + [vmem],
        scratch_shapes=[
            pltpu.VMEM(field, F32),
            pltpu.VMEM(field, F32),
            pltpu.VMEM(field, F32),
            pltpu.VMEM((SX, SY, 4 * FACE, 4 * FACE), BF16),
            pltpu.VMEM((SX, SY, 4 * FACE, 4 * FACE), BF16),
            pltpu.VMEM((SX, SY, 2, FACE), jnp.int32),
            pltpu.VMEM((1, 2 * FACE), F32),
            pltpu.VMEM((SX, SY), F32),
            pltpu.VMEM((2 * FACE, LANES), F32),
            pltpu.VMEM((4, SX + 1, SY, FACE, CASES), BF16),
            pltpu.VMEM((4, SX, SY + 1, FACE, CASES), BF16),
            pltpu.VMEM((2, SX + 1, SY, FACE, CASES), F32),
            pltpu.VMEM((2, SX, SY + 1, FACE, CASES), F32),
            pltpu.VMEM((3, 2, SY, FACE, CASES), BF16),
            pltpu.VMEM((3, 2, SX, FACE, CASES), BF16),
            pltpu.VMEM((3, 2, SY, FACE, CASES), BF16),
            pltpu.VMEM((3, 2, SX, FACE, CASES), BF16),
            pltpu.VMEM((SX, LANES), F32),
            pltpu.VMEM((nz, SX, LANES), F32),
            pltpu.VMEM((2, TILE, LANES), F32),
            pltpu.VMEM((ny, 2, TILE, LANES), F32),
            pltpu.VMEM((2, SX + 1, TILE, LANES), F32),
            pltpu.VMEM((2, nz, SX + 1, TILE, LANES), F32),
            pltpu.VMEM((nz, SX, 2, LANES), F32),
            pltpu.VMEM((SX, 2, LANES), F32),
            pltpu.VMEM((2, group, TILE, LANES), F32),
            pltpu.VMEM((group, TILE, LANES), F32),
            pltpu.VMEM((2, group, TILE, LANES), F32),
            pltpu.VMEM((group, TILE, LANES), F32),
            pltpu.VMEM((2, 3, TILE, LANES), F32),
            pltpu.VMEM((2, ny, 3, TILE, LANES), F32),
            pltpu.VMEM((3, ny, TILE, LANES), F32),
            pltpu.VMEM((2, group + 1, TILE, LANES), F32),
            pltpu.VMEM((2, SX + 1, TILE, LANES), F32),
            pltpu.VMEM((2, SX, 2, LANES), F32),
            pltpu.VMEM((8, LANES), F32),
            pltpu.VMEM((8, LANES), F32),
            pltpu.VMEM((2 * nz, 8, LANES), F32),
            pltpu.VMEM((ny * nc, 8, LANES), F32),
            pltpu.VMEM((2, LANES), F32),
            pltpu.VMEM((2, LANES), F32),
            pltpu.VMEM((2 * nz, 2, LANES), F32),
            pltpu.VMEM((ny * nc, 2, LANES), F32),
            pltpu.SemaphoreType.DMA((11,)),
            pltpu.SemaphoreType.DMA((n_sends,)),
            pltpu.SemaphoreType.DMA((n_sends,)),
        ],
        compiler_params=pltpu.CompilerParams(
            collective_id=0, has_side_effects=True, vmem_limit_bytes=60 << 20
        ),
        cost_estimate=pl.CostEstimate(flops=1_100_000_000, bytes_accessed=6 << 20, transcendentals=8),
    )(load_field, schur_blocks, local_inverse, face_order, coarse_weights.reshape(1, -1), coarse_decay)
    first, second = coef[0:2].reshape(CASES), coef[2:4].reshape(CASES)
    return first * s_field + second * t_field


def solution(mesh):
    nx, ng = mesh.shape["gx"], mesh.shape["gy"]
    nz = 8 if nx % 8 == 0 else 2
    in_specs = (
        P("gx", "gy", None, None),
        P("gx", "gy", None, None),
        P("gx", "gy", None, None),
        P("gx", "gy", None, None),
        P(),
        P("gx", "gy"),
    )
    return jax.shard_map(
        functools.partial(local, (nx // nz, nz, ng)),
        mesh=mesh, in_specs=in_specs, out_specs=P("gx", "gy", None, None), check_vma=False,
    )
```

time: 68.4 us -> 64.1 us (0.937)
  local copies, waits for them, and re-layouts: 5.05 us -> 0.67 us
  other arithmetic: 1.14 us -> 2.65 us
  Pallas kernels: 61.9 us -> 60.6 us
    unnamed x12 -> x2, local copies, waits for them, and re-layouts: 5.05 us -> 0.67 us
    add x1, other arithmetic: 1.14 us -> 2.65 us  [local(): return first * s_field + second * t_field]
    pallas_call x1, Pallas kernels: 61.9 us -> 60.6 us  [local(): pl.pallas_call(functools.partial(kernel, ny, nz, ng), out_shape=[jax.Shap...]
where the time goes in v2:
time: 64.1 us; the launch traced here: 63.9 us
  Pallas kernels  60.6 us (95%)
  other arithmetic  2.65 us (4%)
  local copies, waits for them, and re-layouts  0.67 us (1%)
    pallas_call x1, Pallas kernels, local(): pl.pallas_call(functools.partial(kernel, ny, nz, ng), out_shape=[jax.Shap...  60.6 us
    add x1, other arithmetic, local(): return first * s_field + second * t_field  2.65 us

profile of v2, /device:TPU:1, one launch (start us, length us, event | category | flops | bytes accessed | tf_op | source)
XLA Modules:
  0.0 63.9 jit_solution(12684972575691856254)
XLA Ops:
  0.0 60.6 %shard_map.64 = (f32[2,4,128,256]{3,2,1,0:T(8,128)}, f32[2,4,128,256]{3,2,1,0:T(8,128)}, f32[4,128]{1,0:T(4,128)}) custom-call(f32[2,4,128,256]{3,2,1,0:T(8,128)} %load_hbm.1, bf16[2,4,256,256]{3,2,1,0:T(8,128)(2,1)} %schur_hbm.1, bf16[2,4,256,256]{3,2,1,0:T(8,128)(2,1)} %inverse_hbm.1, s32[2,4,2,64]{3,2,1,0:T(2,128)} %order_hbm.1, f32[1,128]{1,0:T(1,128)} %bitcast.5, ...), custom_call_target="tpu_custom_call" | custom-call | flops 1100000000 | bytes 6291456 | tf_op jit(solution)/shard_map/pallas_call | solution.py:466
  60.6 0.0 copy-start
  60.6 0.7 %copy-done = f32[4,128]{1,0:T(4,128)S(1)} copy-done((f32[4,128]{1,0:T(4,128)S(1)}, f32[4,128]{1,0:T(4,128)}, u32[]{:S(2)}) %copy-start) | copy-done | bytes 2072
  61.3 2.7 %multiply_add_fusion = f32[2,4,128,256]{3,2,1,0:T(8,128)} fusion(f32[2,4,128,256]{3,2,1,0:T(8,128)} %get-tuple-element.10, f32[2,4,128,256]{3,2,1,0:T(8,128)} %get-tuple-element.9, f32[256]{0:T(256)S(1)} %get-tuple-element.12, f32[256]{0:T(256)S(1)} %get-tuple-element.11), kind=kLoop, calls=%fused_computation | loop fusion | flops 786432 | bytes 3147776 | tf_op jit(solution)/shard_map/add | solution.py:529
  (1 shorter events, 0.0 us)
Async XLA Ops:
  60.6 0.7 %copy-start = (f32[4,128]{1,0:T(4,128)S(1)}, f32[4,128]{1,0:T(4,128)}, u32[]{:S(2)}) copy-start(f32[4,128]{1,0:T(4,128)} %get-tuple-element.8) | copy-start | bytes 6148

commit v3 on v2

--- a/solution.py
+++ b/solution.py
@@ -21,7 +21,7 @@
 def kernel(
     ny, nz, ng,
     load_hbm, schur_hbm, inverse_hbm, order_hbm, weight_hbm, decay_hbm,
-    s_hbm, t_hbm, coef_out,
+    x_hbm,
     s_out, t_out, load, blocks_s, blocks_p, order, weight, decay,
     wcol, edge_w, north_w, acc_e, acc_n, send_e, send_n, recv_e, recv_n,
     ksrc, kz, kw, ykw, zsrc, za, zs, south_part, d_all, k_all, climb_l, trans, fg, ybuf, line_in,
@@ -406,7 +406,6 @@
     coarse0 = line_finish(0)
     total1, halo_e, halo_n = stage(1, blocks_s, halo_e, halo_n, 0, s_out)
 
-    s_done = fetch(s_out, s_hbm)
     for b in range(SY):
         rows = slice(2 * b, 2 * b + 2)
         zsrc[1, 0, rows] = weigh(acc_e[1, 0, b], w_east) * west_open
@@ -434,7 +433,6 @@
 
     total3, _, _ = stage(3, blocks_s, halo_e, halo_n, 1, t_out)
     mom3[...] = by_half(total3)
-    t_done = fetch(t_out, t_hbm)
     late = all_sum(mom3, mid3, sum3_a, sum3_b)
     late_a = late[0]()
     early_b = early[1](early_a)
@@ -448,11 +446,18 @@
     mixed = m1 - step0 * m2
     curvature1 = mixed - step0 * m2 + step0 * step0 * m3 + 2.0 * beta * mixed + beta * beta * m1
     step1 = inner1 / curvature1
-    coef_out[0:2] = step0 + step1 * (1.0 + beta)
-    coef_out[2:4] = -step0 * step1
-
-    s_done.wait()
-    t_done.wait()
+    first, second = step0 + step1 * (1.0 + beta), -step0 * step1
+    first = jnp.concatenate([first[0:1], first[1:2]], axis=1)
+    second = jnp.concatenate([second[0:1], second[1:2]], axis=1)
+    written = []
+    for a in range(SX):
+        for b in range(0, SY, 2):
+            for c in (b, b + 1):
+                s_out[a, c] = first * s_out[a, c] + second * t_out[a, c]
+            written.append(fetch(s_out.at[a, b : b + 2], x_hbm.at[a, b : b + 2]))
+
+    for copy in written:
+        copy.wait()
     for copy in sent:
         copy.wait_send()
 
@@ -462,16 +467,11 @@
     nc, group = ng // 2, SX * nz
     n_sends = 1 + 3 * 2 + 7 * (SY // CUT) + 3 * (nz - 1 + ny - 1) + nz + 2 + 2 * (2 * nz - 1 + ny * nc - 1)
     field = (SX, SY, 2 * FACE, CASES)
-    vmem = pl.BlockSpec(memory_space=pltpu.VMEM)
-    s_field, t_field, coef = pl.pallas_call(
+    return pl.pallas_call(
         functools.partial(kernel, ny, nz, ng),
-        out_shape=[
-            jax.ShapeDtypeStruct(field, F32),
-            jax.ShapeDtypeStruct(field, F32),
-            jax.ShapeDtypeStruct((4, LANES), F32),
-        ],
+        out_shape=jax.ShapeDtypeStruct(field, F32),
         in_specs=[pl.BlockSpec(memory_space=pltpu.HBM)] * 6,
-        out_specs=[pl.BlockSpec(memory_space=pltpu.HBM)] * 2 + [vmem],
+        out_specs=pl.BlockSpec(memory_space=pltpu.HBM),
         scratch_shapes=[
             pltpu.VMEM(field, F32),
             pltpu.VMEM(field, F32),
@@ -516,7 +516,7 @@
             pltpu.VMEM((2, LANES), F32),
             pltpu.VMEM((2 * nz, 2, LANES), F32),
             pltpu.VMEM((ny * nc, 2, LANES), F32),
-            pltpu.SemaphoreType.DMA((11,)),
+            pltpu.SemaphoreType.DMA((13,)),
             pltpu.SemaphoreType.DMA((n_sends,)),
             pltpu.SemaphoreType.DMA((n_sends,)),
         ],
@@ -525,8 +525,6 @@
         ),
         cost_estimate=pl.CostEstimate(flops=1_100_000_000, bytes_accessed=6 << 20, transcendentals=8),
     )(load_field, schur_blocks, local_inverse, face_order, coarse_weights.reshape(1, -1), coarse_decay)
-    first, second = coef[0:2].reshape(CASES), coef[2:4].reshape(CASES)
-    return first * s_field + second * t_field
 
 
 def solution(mesh):

time: 64.1 us -> 63.4 us (0.989)
  other arithmetic: 2.65 us -> 0 us
  local copies, waits for them, and re-layouts: 0.67 us -> 2.27 us
    add x1 -> x0, other arithmetic: 2.65 us -> none  [local(): return first * s_field + second * t_field]
    unnamed x2 -> x1, local copies, waits for them, and re-layouts: 0.67 us -> 2.27 us
where the time goes in v3:
time: 63.4 us; the launch traced here: 63.3 us
  Pallas kernels  61 us (96%)
  local copies, waits for them, and re-layouts  2.27 us (4%)
    pallas_call x1, Pallas kernels, local(): pl.pallas_call(functools.partial(kernel, ny, nz, ng), out_shape=jax.Shape...  61 us
    unnamed x1, local copies, waits for them, and re-layouts  2.27 us

profile of v3, /device:TPU:1, one launch (start us, length us, event | category | flops | bytes accessed | tf_op | source)
XLA Modules:
  0.0 63.3 jit_solution(16507306893085396925)
XLA Ops:
  0.0 61.0 %shard_map.64 = f32[2,4,128,256]{3,2,1,0:T(8,128)} custom-call(f32[2,4,128,256]{3,2,1,0:T(8,128)} %load_hbm.1, bf16[2,4,256,256]{3,2,1,0:T(8,128)(2,1)} %schur_hbm.1, bf16[2,4,256,256]{3,2,1,0:T(8,128)(2,1)} %inverse_hbm.1, s32[2,4,2,64]{3,2,1,0:T(2,128)} %order_hbm.1, f32[1,128]{1,0:T(1,128)} %bitcast.1, f32[2,4]{1,0:T(2,128)} %decay_hbm.1), custom_call_target="tpu_custom_call" | custom-call | flops 1100000000 | bytes 6291456 | tf_op jit(solution)/shard_map/pallas_call | solution.py:470
  61.0 2.3 %copy.8 = f32[2,4,128,256]{3,2,1,0:T(8,128)} copy(f32[2,4,128,256]{3,2,1,0:T(8,128)} %shard_map.64) | data formatting | bytes 2097152
